TPU v7x, 512 devices: a whole 4x4x16 slice. The times are simulated.
512 devices in a mesh: sec: 4 (over y), ep: 128 (over x, z, core).
Axes of the slice: x: 4, y: 4, z: 16, core: 2. Of those that a mesh axis runs over, the one named last changes fastest.
Arguments:
- tokens: bfloat16 [2048, 3584], P('ep', 'sec'), may hold values from -6 to 6
- up_weight: bfloat16 [128, 3584, 1024], P('ep', 'sec'), may hold values from -0.09375 to 0.09375
- down_weight: bfloat16 [128, 1024, 3584], P('ep', None, 'sec'), may hold values from -0.1875 to 0.1875
- expert_ids: int32 [2048, 8], P('ep'), may hold values from 0 to 127, all different within a row; in each aligned block of 16 rows (0 to 15, 16 to 31, ...) at most 2 rows name the same one
- route_weight: float32 [2048, 8], P('ep'), may hold values from 0.05 to 1
Outputs:
- combined: bfloat16 [2048, 3584], P('ep', 'sec')
Inputs may be any that keep to these rules, and one draw needn't show every extreme that they name: `expert_ids`: each token names 8 different experts. Among the tokens of one index of ep no expert is named more than 2 times, and that count is reached.
All inputs are finite; a program needn't handle non-finite values.
Results may differ from a plain program's by a relative error of at most 0.0058.
Values may be sent and summed in bfloat16 or wider, within the bound.
A program may use at most 64 MiB of HBM per device.

v0:
```python
import jax
import jax.numpy as jnp
from jax import lax
from jax.sharding import PartitionSpec as P


def body(tokens, up_weight, down_weight, expert_ids, route_weight):
    experts = lax.axis_size("ep")
    row_count, pick_count = expert_ids.shape
    features = tokens.shape[1]
    capacity = max(2, min(row_count, 2 * row_count * pick_count // experts))
    flat_ids = expert_ids.reshape(-1)
    one_hot = (flat_ids[:, None] == jnp.arange(experts, dtype=jnp.int32)[None, :]).astype(jnp.int32)
    earlier = jnp.sum((jnp.cumsum(one_hot, axis=0) - one_hot) * one_hot, axis=1)
    slot_ids = flat_ids * capacity + earlier
    dispatch = (
        slot_ids[:, None] == jnp.arange(experts * capacity, dtype=jnp.int32)[None, :]
    ).astype(jnp.bfloat16)
    repeated = jnp.repeat(tokens, pick_count, axis=0)
    outgoing = lax.dot_general(
        dispatch, repeated, (((0,), (0,)), ((), ())), preferred_element_type=jnp.float32
    )
    outgoing = outgoing.astype(jnp.bfloat16).reshape(experts, capacity, features)
    arrived = lax.all_to_all(outgoing, "ep", split_axis=0, concat_axis=0, tiled=True).reshape(
        experts * capacity, features
    )
    partial_up = jnp.dot(arrived, up_weight[0], preferred_element_type=jnp.float32)
    upper = lax.psum(partial_up, "sec")
    activated = jax.nn.silu(upper).astype(jnp.bfloat16)
    expert_out = jnp.dot(activated, down_weight[0], preferred_element_type=jnp.float32).astype(
        jnp.bfloat16
    )
    expert_out = expert_out.reshape(experts, capacity, features)
    received = lax.all_to_all(expert_out, "ep", split_axis=0, concat_axis=0, tiled=True).reshape(
        experts * capacity, features
    )
    picked = jnp.dot(dispatch, received, preferred_element_type=jnp.float32)
    scale = 2.5 * route_weight / jnp.sum(route_weight, axis=1, keepdims=True)
    combined = jnp.sum(picked.reshape(row_count, pick_count, features) * scale[:, :, None], axis=1)
    return combined.astype(jnp.bfloat16)


def solution(mesh):
    placed = (
        P("ep", "sec"),
        P("ep", "sec", None),
        P("ep", None, "sec"),
        P("ep", None),
        P("ep", None),
    )
    return jax.shard_map(
        body, mesh=mesh, in_specs=placed, out_specs=P("ep", "sec"), check_vma=False
    )
```

profile of v0, /device:TPU:6, one launch (start us, length us, event | category | flops | bytes accessed | tf_op | source)
XLA Modules:
  0.0 172.4 jit_solution(10529603074885498548)
XLA Ops:
  6.5 0.0 copy-start
  6.5 0.0 all-reduce.2.cloned.1.call-start
  6.5 0.9 copy.9
  7.4 0.1 eq.50
  7.5 0.1 fusion.15
  7.6 0.2 reduce_window_sum.11
  7.8 0.2 select_reduce_fusion
  8.0 1.1 convolution_convert_fusion
  9.1 0.2 reshape.53
  9.3 49.0 %all_to_all.10 = bf16[128,2,896]{2,1,0:T(2,128)(2,1)S(1)} all-to-all(bf16[128,2,896]{2,1,0:T(2,128)(2,1)S(1)} %reshape.53), channel_id=1, replica_groups=mesh['sec'=4,'ep'=128] {'ep'}, dimensions={0} | all-to-all | bytes 917504 | tf_op jit(solution)/shard_map/all_to_all | solution.py:24
  58.4 0.2 reshape.54
  58.5 0.0 copy-done
  58.5 1.8 %fusion.2 = f32[256,1024]{1,0:T(8,128)} fusion(bf16[256,896]{1,0:T(8,128)(2,1)S(1)} %reshape.54, bf16[1,896,1024]{2,1,0:T(8,128)(2,1)S(1)} %copy-done), kind=kOutput, calls=%fused_computation.2 | convolution fusion | flops 469762048 | bytes 3342336 | tf_op jit(solution)/shard_map/dot_general | solution.py:27
  60.3 0.0 all-reduce.2.cloned.1.call-update
  60.3 54.1 %all-reduce.2.cloned.1.call-done = f32[256,1024]{1,0:T(8,128)} async-done(((f32[256,1024]{1,0:T(8,128)}), f32[256,1024]{1,0:T(8,128)}) %all-reduce.2.cloned.1.call-update) | async-done | bytes 1048592 | tf_op jit(solution)/shard_map/psum | solution.py:28
  114.5 2.6 %fusion.4 = bf16[256,896]{1,0:T(8,128)(2,1)S(1)} fusion(bf16[1,1024,896]{2,1,0:T(8,128)(2,1)} %param.7, f32[256,1024]{1,0:T(8,128)} %all-reduce.2.cloned.1.call-done), kind=kOutput, calls=%fused_computation.4 | convolution fusion | flops 471302144 | bytes 3342336 | tf_op jit(solution)/shard_map/dot_general | solution.py:30
  117.0 0.0 copy-start.1
  117.1 0.9 reshape.55
  118.0 17.0 %all-to-all-start.1 = ((bf16[128,2,896]{2,1,0:T(2,128)(2,1)}), bf16[128,2,896]{2,1,0:T(2,128)(2,1)S(1)}, u32[]{:S(2)}, u32[]{:S(2)}) async-start(bf16[128,2,896]{2,1,0:T(2,128)(2,1)} %reshape.55), calls=%async_computation.1 | async-start | bytes 917504 | tf_op jit(solution)/shard_map/all_to_all | solution.py:34
  135.0 0.1 reduce_sum.30
  135.1 0.0 copy-done.1
  135.2 0.1 copy.11
  135.2 29.1 %all-to-all-done.1 = bf16[128,2,896]{2,1,0:T(2,128)(2,1)S(1)} async-done(((bf16[128,2,896]{2,1,0:T(2,128)(2,1)}), bf16[128,2,896]{2,1,0:T(2,128)(2,1)S(1)}, u32[]{:S(2)}, u32[]{:S(2)}) %all-to-all-start.1) | async-done | bytes 458784 | tf_op jit(solution)/shard_map/all_to_all | solution.py:34
  164.4 0.2 reshape.57
  164.6 1.0 fusion.7
  (4 shorter events, 0.0 us)
Async XLA Ops:
  6.5 52.0 %copy-start = (bf16[1,896,1024]{2,1,0:T(8,128)(2,1)S(1)}, bf16[1,896,1024]{2,1,0:T(8,128)(2,1)}, u32[]{:S(2)}) copy-start(bf16[1,896,1024]{2,1,0:T(8,128)(2,1)} %param.6) | copy-start | bytes 5505028
  6.5 107.9 %all-reduce.2.cloned.1.call-start = ((), (), s32[]{:S(2)}) async-start(), calls=%async_computation.2 | async-start | bytes 2097152 | tf_op jit(solution)/shard_map/psum | solution.py:28
  117.0 18.1 %copy-start.1 = (f32[16,8]{0,1:T(8,128)S(1)}, f32[16,8]{0,1:T(8,128)}, u32[]{:S(2)}) copy-start(f32[16,8]{0,1:T(8,128)} %param.9) | copy-start | bytes 1540
  118.0 46.4 %all-to-all-start.1 = ((bf16[128,2,896]{2,1,0:T(2,128)(2,1)}), bf16[128,2,896]{2,1,0:T(2,128)(2,1)S(1)}, u32[]{:S(2)}, u32[]{:S(2)}) async-start(bf16[128,2,896]{2,1,0:T(2,128)(2,1)} %reshape.55), calls=%async_computation.1 | async-start | bytes 917504 | tf_op jit(solution)/shard_map/all_to_all | solution.py:34
Sparse Core Ops, SparseCore 0:
  60.5 53.9 all-reduce.1
where the time goes:
time: 174 us; the launch traced here: 172 us
  waiting for transfers between devices  83.3 us (48%)
  blocking collectives  49 us (28%)
  starting transfers between devices  17 us (10%)
  between operations  13.5 us (8%)
  matrix products  6.44 us (4%)
  local copies, waits for them, and re-layouts  2.6 us (1%)
    psum x1, waiting for transfers between devices, body(): upper = lax.psum(partial_up, 'sec')  54.1 us
    all_to_all x1, blocking collectives, body(): lax.all_to_all(outgoing, 'ep', split_axis=0, concat_axis=0, tiled=True)  49 us
    all_to_all x1, waiting for transfers between devices, body(): lax.all_to_all(expert_out, 'ep', split_axis=0, concat_axis=0, tiled=True)  29.1 us
    all_to_all x1, starting transfers between devices, body(): lax.all_to_all(expert_out, 'ep', split_axis=0, concat_axis=0, tiled=True)  17 us
  transfers between devices with their start and end apart: 2, of which 2 were waited for; matrix products, arithmetic and copies ran while one was open for 0% of the time, Pallas kernels for 0%

commit v1 on v0

v1 whole, which is shorter than its diff:
```python
import functools

import jax
import jax.numpy as jnp
from jax import lax
from jax.experimental import pallas as pl
from jax.experimental.pallas import tpu as pltpu
from jax.sharding import PartitionSpec as P

MESH = pl.DeviceIdType.MESH
F32, BF16 = jnp.float32, jnp.bfloat16
NX, NY, NZ, NC = 4, 4, 16, 2
ROWS, TOP, CAP = 16, 8, 2
PLANE = NX * NC
ORDER = (0, 1, -1, 3, -3, 2, -2, 4, -4, 5, -5, 6, -6, 7, -7, 8)
PLACE = {o: i for i, o in enumerate(ORDER)}
FAR = (6, -6, 3, -3)
NEAR = tuple((a, b, 0) for a in (0, 3, -3, 6, -6) for b in (1, -1)) + ((6, 2, 1), (-6, -2, 2))
EARLY = tuple(a + b for a, b, _ in NEAR if a in (0, 3, -3))
PEERS_Z = (6, -6, 3, -3, 1, -1, 2, -2)


def offset(a, b):
    o = a + b
    return 8 if o == -8 else o


def columns(part, width):
    return pl.ds(0, width) if part == 0 else pl.ds(0, 512) if part == 1 else pl.ds(512, width - 512)


def kernel(
    tok_hbm, up_hbm, down_hbm, ids_ref, weight_ref, out_ref,
    up_v, down_v, tok, sel, xin, pup, rup, own, act, eout, ret, mix, par, par32, brecv, qs, qr,
    load_sem, far_s, far_r, near_s, near_r, x_s, x_r, rs_s, rs_r, ag_s, ag_r, b_s, b_r, bn_s, bn_r, q_s, q_r,
):
    y = lax.axis_index("sec")
    ep = lax.axis_index("ep")
    core = lax.rem(ep, NC)
    z = lax.rem(ep // NC, NZ)
    x = ep // (NC * NZ)
    width = tok_hbm.shape[1]
    total = tok.shape[1]
    quarter = rup.shape[3]

    def along_z(step):
        return (y, (x * NZ + lax.rem(z + step + NZ, NZ)) * NC + core)

    def in_plane(j):
        return (y, (lax.rem(x + j // NC, NX) * NZ + z) * NC + lax.rem(core + j % NC, NC))

    def along_y(d):
        return (lax.rem(y + d, NY), ep)

    def back(j):
        return ((NX - j // NC) % NX) * NC + j % NC

    def send(src, dst, s, r, to):
        copy = pltpu.make_async_remote_copy(
            src_ref=src, dst_ref=dst, send_sem=s, recv_sem=r, device_id=to, device_id_type=MESH
        )
        copy.start()
        return copy

    def block(o):
        return pl.ds(PLACE[o] * ROWS, ROWS)

    loads = [
        pltpu.make_async_copy(tok_hbm, tok.at[block(0), pl.ds(0, width)], load_sem.at[0]),
        pltpu.make_async_copy(up_hbm, up_v, load_sem.at[1]),
        pltpu.make_async_copy(down_hbm, down_v, load_sem.at[2]),
    ]
    for load in loads:
        load.start()
    barrier = pltpu.get_barrier_semaphore()
    peers = [along_z(s) for s in PEERS_Z] + [in_plane(j) for j in range(1, PLANE)] + [along_y(d) for d in range(1, NY)]
    for peer in peers:
        pl.semaphore_signal(barrier, inc=1, device_id=peer, device_id_type=MESH)

    ids = ids_ref[...]
    lanes = ids.shape[1]
    number = lax.broadcasted_iota(jnp.int32, (128, lanes), 0)
    hits = [number == ids[k : k + 1, :] for k in range(TOP)]
    named = sum(jnp.where(h, 1.0, 0.0) for h in hits).astype(BF16)
    before = lax.broadcasted_iota(jnp.int32, (lanes, lanes), 0) < lax.broadcasted_iota(jnp.int32, (lanes, lanes), 1)
    earlier = jnp.dot(named, jnp.where(before, 1.0, 0.0).astype(BF16), preferred_element_type=F32)
    slot = jnp.concatenate([jnp.sum(jnp.where(h, earlier, 0.0), axis=0, keepdims=True) for h in hits], axis=0)
    code = 2.0 * ids.astype(F32) + slot
    weight = weight_ref[...]
    scale = 2.5 * weight / jnp.sum(weight, axis=0, keepdims=True)
    high = scale.astype(BF16).astype(F32)
    middle = (scale - high).astype(BF16).astype(F32)
    low = scale - high - middle
    table = jnp.concatenate([code, high, middle, low, jnp.zeros((128 - 4 * TOP, lanes), F32)], axis=0).astype(BF16)
    unit = lax.broadcasted_iota(jnp.int32, (ROWS, lanes), 0) == lax.broadcasted_iota(jnp.int32, (ROWS, lanes), 1)
    loads[0].wait()
    tok[block(0), pl.ds(width, total - width)] = lax.dot_general(
        jnp.where(unit, 1.0, 0.0).astype(BF16), table, (((1,), (1,)), ((), ())), preferred_element_type=F32
    ).astype(BF16)

    pl.semaphore_wait(barrier, len(peers))

    far = {}
    for i, a in enumerate(FAR):
        far[a] = send(tok.at[block(0)], tok.at[block(a)], far_s.at[i], far_r.at[i], along_z(a))
    near = {}

    def forward(a):
        for i, (held, b, part) in enumerate(NEAR):
            if held == a:
                cols = columns(part, total)
                near[i] = send(
                    tok.at[block(a), cols], tok.at[block(offset(a, b)), cols], near_s.at[i], near_r.at[i], along_z(b)
                )

    forward(0)
    for a in (3, -3, 6, -6):
        far[a].wait_recv()
        forward(a)

    row = lax.broadcasted_iota(jnp.int32, (128, 128), 0)
    lane = lax.broadcasted_iota(jnp.int32, (128, 128), 1)
    relative = row // (TOP * CAP)
    expert = (lax.rem(x + relative // NC, NX) * NZ + z) * NC + lax.rem(core + lax.rem(relative, NC), NC)
    wanted = (CAP * expert + lax.rem(row, CAP)).astype(F32)
    same = lax.rem(row // CAP, TOP) == lane // ROWS
    turn = jnp.where(row == lane, 1.0, 0.0).astype(BF16)[: 4 * TOP]

    def pick(q):
        codes = lax.dot_general(
            turn, tok[pl.ds(q * 128, 128), pl.ds(width, total - width)], (((1,), (1,)), ((), ())),
            preferred_element_type=F32,
        )
        chosen = jnp.zeros((128, 128), F32)
        scaled = jnp.zeros((128, 128), F32)
        for k in range(TOP):
            match = same & (wanted == codes[k : k + 1, :])
            value = codes[TOP + k : TOP + k + 1, :] + codes[2 * TOP + k : 2 * TOP + k + 1, :]
            value = value + codes[3 * TOP + k : 3 * TOP + k + 1, :]
            chosen = jnp.where(match, 1.0, chosen)
            scaled = jnp.where(match, value, scaled)
        rows = jnp.dot(chosen.astype(BF16), tok[pl.ds(q * 128, 128), pl.ds(0, width)], preferred_element_type=F32)
        sel[q] = rows.astype(BF16)
        xin[q, pl.ds(0, ROWS)] = sel[q, pl.ds(0, ROWS)]
        copies = []
        for j in (4, 5, 2, 6, 3, 7, 1):
            copies.append(
                send(
                    sel.at[q, pl.ds(j * ROWS, ROWS)], xin.at[q, pl.ds(back(j) * ROWS, ROWS)],
                    x_s.at[q, j], x_r.at[q, back(j)], in_plane(j),
                )
            )
        turned = jnp.transpose(scaled)
        first = turned.astype(BF16)
        second = (turned - first.astype(F32)).astype(BF16)
        third = (turned - first.astype(F32) - second.astype(F32)).astype(BF16)
        mix[q, 0] = first
        mix[q, 1] = second
        mix[q, 2] = third
        return copies

    def arrive(q):
        for i, (a, b, _) in enumerate(NEAR):
            if PLACE[offset(a, b)] // 8 == q:
                near[i].wait_recv()

    arrive(0)
    x0 = pick(0)
    arrive(1)
    x1 = pick(1)
    picked = [x0, x1]
    loads[1].wait()
    loads[2].wait()

    sums = [None, None]
    for q in range(2):
        for copy in picked[q]:
            copy.wait_recv()
        sums[q] = []
        for d in (2, 1, 3, 0):
            cols = pl.ds(pl.multiple_of(lax.rem(y + d, NY) * quarter, quarter), quarter)
            part = jnp.dot(xin[q], up_v[:, cols], preferred_element_type=F32)
            if d == 0:
                own[q] = part
            else:
                pup[q, d] = part.astype(BF16)
                sums[q].append(
                    send(pup.at[q, d], rup.at[q, NY - d], rs_s.at[q, d], rs_r.at[q, NY - d], along_y(d))
                )
    gathered = [None, None]
    for q in range(2):
        for copy in sums[q]:
            copy.wait_recv()
        upper = own[q] + rup[q, 1].astype(F32) + rup[q, 2].astype(F32) + rup[q, 3].astype(F32)
        act[q, 0] = (upper / (1.0 + jnp.exp(-upper))).astype(BF16)
        gathered[q] = [
            send(act.at[q, 0], act.at[q, NY - d], ag_s.at[q, d], ag_r.at[q, NY - d], along_y(d)) for d in (2, 1, 3)
        ]
    returned = [None, None]
    for q in range(2):
        for copy in gathered[q]:
            copy.wait_recv()
        result = jnp.zeros((128, width), F32)
        for r in range(NY):
            hidden = pl.ds(pl.multiple_of(lax.rem(y + r, NY) * quarter, quarter), quarter)
            result = result + jnp.dot(act[q, r], down_v[hidden, :], preferred_element_type=F32)
        eout[q] = result.astype(BF16)
        ret[q, pl.ds(0, ROWS)] = eout[q, pl.ds(0, ROWS)]
        returned[q] = [
            send(
                eout.at[q, pl.ds(j * ROWS, ROWS)], ret.at[q, pl.ds(back(j) * ROWS, ROWS)],
                b_s.at[q, j], b_r.at[q, back(j)], in_plane(j),
            )
            for j in (4, 5, 2, 6, 3, 7, 1)
        ]

    homeward = {}
    for q in range(2):
        for copy in returned[q]:
            copy.wait_recv()
        rows = ret[q]
        part = jnp.dot(mix[q, 0], rows, preferred_element_type=F32)
        part = part + jnp.dot(mix[q, 1], rows, preferred_element_type=F32)
        part = part + jnp.dot(mix[q, 2], rows, preferred_element_type=F32)
        par32[q] = part
        par[pl.ds(q * 128, 128)] = part.astype(BF16)
        for i, (a, b, half) in enumerate(NEAR):
            o = offset(a, b)
            if PLACE[o] // 8 == q:
                cols = columns(half, width)
                homeward[i] = send(
                    par.at[block(o), cols], brecv.at[i, :, cols], bn_s.at[i], bn_r.at[i], along_z(-b)
                )
    last = {}
    kept = None
    for a in (6, -6, 3, -3, 0):
        chunk, start = divmod(PLACE[a] * ROWS, 128)
        value = par32[chunk, pl.ds(start, ROWS)]
        for i, (held, b, half) in enumerate(NEAR):
            if held == a:
                homeward[i].wait_recv()
                if half == 0:
                    value = value + brecv[i].astype(F32)
                elif half == 1:
                    value = value + jnp.concatenate(
                        [brecv[i, :, pl.ds(0, 512)].astype(F32), jnp.zeros((ROWS, width - 512), F32)], axis=1
                    )
                else:
                    value = value + jnp.concatenate(
                        [jnp.zeros((ROWS, 512), F32), brecv[i, :, pl.ds(512, width - 512)].astype(F32)], axis=1
                    )
        if a == 0:
            kept = value
        else:
            i = FAR.index(a)
            qs[i] = value.astype(BF16)
            last[a] = send(qs.at[i], qr.at[i], q_s.at[i], q_r.at[i], along_z(-a))
    for a in (3, -3, 6, -6):
        last[a].wait_recv()
        kept = kept + qr[FAR.index(a)].astype(F32)
    out_ref[...] = kept.astype(BF16)

    started = list(far.values()) + list(near.values()) + list(homeward.values()) + list(last.values())
    for group in (picked, sums, gathered, returned):
        started += group[0] + group[1]
    for copy in started:
        copy.wait_send()


def body(tokens, up_weight, down_weight, expert_ids, route_weight):
    width = tokens.shape[1]
    hidden = up_weight.shape[2]
    quarter = hidden // NY
    dma = pltpu.SemaphoreType.DMA
    vmem = pl.BlockSpec(memory_space=pltpu.VMEM)
    anywhere = pl.BlockSpec(memory_space=pl.ANY)
    scratch = [
        pltpu.VMEM((width, hidden), BF16),
        pltpu.VMEM((hidden, width), BF16),
        pltpu.VMEM((256, width + 128), BF16),
        pltpu.VMEM((2, 128, width), BF16),
        pltpu.VMEM((2, 128, width), BF16),
        pltpu.VMEM((2, NY, 128, quarter), BF16),
        pltpu.VMEM((2, NY, 128, quarter), BF16),
        pltpu.VMEM((2, 128, quarter), F32),
        pltpu.VMEM((2, NY, 128, quarter), BF16),
        pltpu.VMEM((2, 128, width), BF16),
        pltpu.VMEM((2, 128, width), BF16),
        pltpu.VMEM((2, 3, 128, 128), BF16),
        pltpu.VMEM((256, width), BF16),
        pltpu.VMEM((2, 128, width), F32),
        pltpu.VMEM((len(NEAR), ROWS, width), BF16),
        pltpu.VMEM((len(FAR), ROWS, width), BF16),
        pltpu.VMEM((len(FAR), ROWS, width), BF16),
        dma((3,)),
        dma((len(FAR),)), dma((len(FAR),)),
        dma((len(NEAR),)), dma((len(NEAR),)),
        dma((2, PLANE)), dma((2, PLANE)),
        dma((2, NY)), dma((2, NY)),
        dma((2, NY)), dma((2, NY)),
        dma((2, PLANE)), dma((2, PLANE)),
        dma((len(NEAR),)), dma((len(NEAR),)),
        dma((len(FAR),)), dma((len(FAR),)),
    ]
    return pl.pallas_call(
        kernel,
        out_shape=jax.ShapeDtypeStruct(tokens.shape, BF16),
        in_specs=[anywhere, anywhere, anywhere, vmem, vmem],
        out_specs=vmem,
        scratch_shapes=scratch,
        compiler_params=pltpu.CompilerParams(
            collective_id=0, has_side_effects=True, vmem_limit_bytes=48 * 2**20
        ),
        cost_estimate=pl.CostEstimate(flops=2 * 2 * 256 * width * hidden, bytes_accessed=4 * width * hidden, transcendentals=0),
        name="experts",
    )(tokens, up_weight[0], down_weight[0], expert_ids.T, route_weight.T)


def solution(mesh):
    placed = (
        P("ep", "sec"),
        P("ep", "sec", None),
        P("ep", None, "sec"),
        P("ep", None),
        P("ep", None),
    )
    return jax.shard_map(
        body, mesh=mesh, in_specs=placed, out_specs=P("ep", "sec"), check_vma=False
    )
```

time: 174 us -> 72.6 us (0.42)
  waiting for transfers between devices: 83.3 us -> 0 us
  Pallas kernels: 0 us -> 66.6 us
  blocking collectives: 49 us -> 0 us
  starting transfers between devices: 17 us -> 0 us
  between operations: 13.5 us -> 0.01 us
  matrix products: 6.44 us -> 0 us
  local copies, waits for them, and re-layouts: 2.6 us -> 5.73 us
    pallas_call x0 -> x1, Pallas kernels: none -> 66.6 us  [body(): pl.pallas_call(kernel, out_shape=jax.ShapeDtypeStruct(tokens.shape, BF16)...]
    psum x1 -> x0, waiting for transfers between devices: 54.1 us -> none  [body(): upper = lax.psum(partial_up, 'sec')]
    all_to_all x1 -> x0, blocking collectives: 49 us -> none  [body(): lax.all_to_all(outgoing, 'ep', split_axis=0, concat_axis=0, tiled=True)]
    all_to_all x1 -> x0, waiting for transfers between devices: 29.1 us -> none  [body(): lax.all_to_all(expert_out, 'ep', split_axis=0, concat_axis=0, tiled=True)]
    all_to_all x1 -> x0, starting transfers between devices: 17 us -> none  [body(): lax.all_to_all(expert_out, 'ep', split_axis=0, concat_axis=0, tiled=True)]
    dot_general x4 -> x0, matrix products: 6.44 us -> none  [the longest x1 2.56 us: body(): jnp.dot(activated, down_weight[0], preferred_element_type=jnp.float32)]
    unnamed x5 -> x11, local copies, waits for them, and re-layouts: 0.9 us -> 5.73 us
  transfers between devices with their start and end apart: 2 -> 0, of which waited for: 2 -> 0; matrix products, arithmetic and copies ran while one was open for 0% -> 0% of each run, Pallas kernels for 0% -> 0%
where the time goes in v1:
time: 72.6 us; the launch traced here: 72.3 us
  Pallas kernels  66.6 us (92%)
  local copies, waits for them, and re-layouts  5.73 us (8%)
    pallas_call x1, Pallas kernels, body(): pl.pallas_call(kernel, out_shape=jax.ShapeDtypeStruct(tokens.shape, BF16)...  66.6 us
    unnamed x11, local copies, waits for them, and re-layouts  5.73 us

profile of v1, /device:TPU:6, one launch (start us, length us, event | category | flops | bytes accessed | tf_op | source)
XLA Modules:
  0.0 72.3 jit_solution(14021305668054156392)
XLA Ops:
  0.0 0.0 copy-start
  0.0 1.5 %copy-done = bf16[1,896,1024]{2,1,0:T(8,128)(2,1)S(1)} copy-done((bf16[1,896,1024]{2,1,0:T(8,128)(2,1)S(1)}, bf16[1,896,1024]{2,1,0:T(8,128)(2,1)}, u32[]{:S(2)}) %copy-start) | copy-done | bytes 1835032
  1.5 0.0 copy-start.1
  1.5 1.5 %copy-done.1 = bf16[1,1024,896]{2,1,0:T(8,128)(2,1)S(1)} copy-done((bf16[1,1024,896]{2,1,0:T(8,128)(2,1)S(1)}, bf16[1,1024,896]{2,1,0:T(8,128)(2,1)}, u32[]{:S(2)}) %copy-start.1) | copy-done | bytes 1835032
  3.0 0.0 copy-start.2
  3.0 0.7 %copy-done.2 = bf16[16,896]{1,0:T(8,128)(2,1)S(1)} copy-done((bf16[16,896]{1,0:T(8,128)(2,1)S(1)}, bf16[16,896]{1,0:T(8,128)(2,1)}, u32[]{:S(2)}) %copy-start.2) | copy-done | bytes 28696
  3.7 0.0 copy-start.3
  3.8 0.7 copy-done.3
  4.4 0.0 copy-start.4
  4.4 0.7 copy-done.4
  5.1 66.6 %experts.1 = bf16[16,896]{1,0:T(8,128)(2,1)S(1)} custom-call(bf16[16,896]{1,0:T(8,128)(2,1)S(1)} %copy-done.2, bf16[896,1024]{1,0:T(8,128)(2,1)S(1)} %bitcast.4, bf16[1024,896]{1,0:T(8,128)(2,1)S(1)} %bitcast.5, s32[8,16]{1,0:T(8,128)S(1)} %bitcast.6, f32[8,16]{1,0:T(8,128)S(1)} %bitcast.7), custom_call_target="tpu_custom_call" | custom-call | flops 939524096 | bytes 3670016 | tf_op jit(solution)/shard_map/experts/pallas_call | solution.py:305
  71.7 0.6 copy.7
Async XLA Ops:
  0.0 1.5 %copy-start = (bf16[1,896,1024]{2,1,0:T(8,128)(2,1)S(1)}, bf16[1,896,1024]{2,1,0:T(8,128)(2,1)}, u32[]{:S(2)}) copy-start(bf16[1,896,1024]{2,1,0:T(8,128)(2,1)} %param.6) | copy-start | bytes 5505028
  1.5 1.5 %copy-start.1 = (bf16[1,1024,896]{2,1,0:T(8,128)(2,1)S(1)}, bf16[1,1024,896]{2,1,0:T(8,128)(2,1)}, u32[]{:S(2)}) copy-start(bf16[1,1024,896]{2,1,0:T(8,128)(2,1)} %param.7) | copy-start | bytes 5505028
  3.0 0.7 %copy-start.2 = (bf16[16,896]{1,0:T(8,128)(2,1)S(1)}, bf16[16,896]{1,0:T(8,128)(2,1)}, u32[]{:S(2)}) copy-start(bf16[16,896]{1,0:T(8,128)(2,1)} %tok_hbm.1) | copy-start | bytes 86020
  3.7 0.7 copy-start.3
  4.4 0.7 copy-start.4

commit v2 on v1

v2 whole, which is shorter than its diff:
```python
import functools

import jax
import jax.numpy as jnp
from jax import lax
from jax.experimental import pallas as pl
from jax.experimental.pallas import tpu as pltpu
from jax.sharding import PartitionSpec as P

MESH = pl.DeviceIdType.MESH
F32, BF16 = jnp.float32, jnp.bfloat16
NX, NY, NZ, NC = 4, 4, 16, 2
ROWS, TOP, CAP = 16, 8, 2
PLANE = NX * NC
ORDER = (-4, 5, -5, 6, -6, 7, -7, 8, 0, 1, -1, 3, -3, 2, -2, 4)
PLACE = {o: i for i, o in enumerate(ORDER)}
META = 128
BLOCK_CUT = ((0, 512), (512, 512))
OUT_CUT = ((0, 384), (384, 512))
HOME_CUT = ((0, 512), (512, 384))


def stages(cuts):
    parts = range(len(cuts))
    far = tuple((a, b, s) for a, b in ((0, 3), (0, -3), (3, 3), (-3, -3)) for s in parts)
    near = tuple((a, b, s) for a in (0, 3, -3, 6, -6) for b in (1, -1) for s in parts)
    return far, near + ((6, 2, 0), (-6, -2, 1))


FAR_OUT, NEAR_OUT = stages(BLOCK_CUT)
FAR_HOME, NEAR_HOME = stages(HOME_CUT)
PEERS_Z = (3, -3, 2, -2, 1, -1)
PEERS_PLANE = (4, 5, 2, 6, 3, 7, 1)
PEERS_Y = (2, 1, 3)


def offset(a, b):
    o = a + b
    return 8 if o == -8 else o


def kernel(
    tok_hbm, up_hbm, down_hbm, ids_hbm, weight_hbm, out_ref,
    ids_ref, weight_ref, up_v, down_v, tok, sel, xin, upacc, pup, rup, act, eout, ret, mix, par, par32, brecv, qs, qr,
    load_sem, far_s, far_r, near_s, near_r, x_s, x_r, rs_s, rs_r, ag_s, ag_r, b_s, b_r, bn_s, bn_r, q_s, q_r,
):
    y = lax.axis_index("sec")
    ep = lax.axis_index("ep")
    core = lax.rem(ep, NC)
    z = lax.rem(ep // NC, NZ)
    x = ep // (NC * NZ)
    width = tok_hbm.shape[1]
    quarter = rup.shape[3]
    live = []

    def along_z(step):
        return (y, (x * NZ + lax.rem(z + step + NZ, NZ)) * NC + core)

    def in_plane(j):
        return (y, (lax.rem(x + j // NC, NX) * NZ + z) * NC + lax.rem(core + j % NC, NC))

    def along_y(d):
        return (lax.rem(y + d, NY), ep)

    def back(j):
        return ((NX - j // NC) % NX) * NC + j % NC

    def send(src, dst, s, r, to):
        copy = pltpu.make_async_remote_copy(
            src_ref=src, dst_ref=dst, send_sem=s, recv_sem=r, device_id=to, device_id_type=MESH
        )
        copy.start()
        live.append(copy)
        return copy

    def block(o):
        return pl.ds(PLACE[o] * ROWS, ROWS)

    loads = [
        pltpu.make_async_copy(ids_hbm, ids_ref, load_sem.at[3]),
        pltpu.make_async_copy(weight_hbm, weight_ref, load_sem.at[4]),
        pltpu.make_async_copy(tok_hbm, tok.at[block(0), pl.ds(META, width)], load_sem.at[0]),
        pltpu.make_async_copy(up_hbm, up_v, load_sem.at[1]),
        pltpu.make_async_copy(down_hbm, down_v, load_sem.at[2]),
    ]
    barrier = pltpu.get_barrier_semaphore()
    peers = [along_z(s) for s in PEERS_Z] + [in_plane(j) for j in PEERS_PLANE] + [along_y(d) for d in PEERS_Y]
    for peer in peers:
        pl.semaphore_signal(barrier, inc=1, device_id=peer, device_id_type=MESH)
    for load in loads:
        load.start()

    loads[0].wait()
    loads[1].wait()
    ids = ids_ref[...]
    lanes = ids.shape[1]
    number = lax.broadcasted_iota(jnp.int32, (128, lanes), 0)
    hits = [number == ids[k : k + 1, :] for k in range(TOP)]
    named = sum(jnp.where(h, 1.0, 0.0) for h in hits).astype(BF16)
    before = lax.broadcasted_iota(jnp.int32, (lanes, lanes), 0) < lax.broadcasted_iota(jnp.int32, (lanes, lanes), 1)
    earlier = jnp.dot(named, jnp.where(before, 1.0, 0.0).astype(BF16), preferred_element_type=F32)
    slot = jnp.concatenate([jnp.sum(jnp.where(h, earlier, 0.0), axis=0, keepdims=True) for h in hits], axis=0)
    code = 2.0 * ids.astype(F32) + slot
    weight = weight_ref[...]
    scale = 2.5 * weight / jnp.sum(weight, axis=0, keepdims=True)
    high = scale.astype(BF16).astype(F32)
    middle = (scale - high).astype(BF16).astype(F32)
    low = scale - high - middle
    table = jnp.concatenate([code, high, middle, low, jnp.zeros((META - 4 * TOP, lanes), F32)], axis=0).astype(BF16)
    unit = lax.broadcasted_iota(jnp.int32, (ROWS, lanes), 0) == lax.broadcasted_iota(jnp.int32, (ROWS, lanes), 1)
    tok[block(0), pl.ds(0, META)] = lax.dot_general(
        jnp.where(unit, 1.0, 0.0).astype(BF16), table, (((1,), (1,)), ((), ())), preferred_element_type=F32
    ).astype(BF16)
    loads[2].wait()
    pl.semaphore_wait(barrier, len(peers))

    far, near = {}, {}

    def step(table, i, entry, s_sem, r_sem):
        a, b, s = entry
        cols = pl.ds(*BLOCK_CUT[s])
        table[entry] = send(
            tok.at[block(a), cols], tok.at[block(offset(a, b)), cols], s_sem.at[i], r_sem.at[i], along_z(b)
        )

    def forward(a, s, q):
        for i, entry in enumerate(FAR_OUT):
            if entry[0] == a and entry[2] == s and q == 0:
                step(far, i, entry, far_s, far_r)
        for i, entry in enumerate(NEAR_OUT):
            if entry[0] == a and entry[2] == s and PLACE[offset(entry[0], entry[1])] // 8 == q:
                step(near, i, entry, near_s, near_r)

    def arrive(q, s):
        for entry in NEAR_OUT:
            if PLACE[offset(entry[0], entry[1])] // 8 == q and entry[2] == s:
                near[entry].wait_recv()

    row = lax.broadcasted_iota(jnp.int32, (128, 128), 0)
    lane = lax.broadcasted_iota(jnp.int32, (128, 128), 1)
    relative = row // (TOP * CAP)
    expert = (lax.rem(x + relative // NC, NX) * NZ + z) * NC + lax.rem(core + lax.rem(relative, NC), NC)
    wanted = (CAP * expert + lax.rem(row, CAP)).astype(F32)
    same = lax.rem(row // CAP, TOP) == lane // ROWS
    turn = jnp.where(row == lane, 1.0, 0.0).astype(BF16)[: 4 * TOP]

    def match(q):
        codes = lax.dot_general(
            turn, tok[pl.ds(q * 128, 128), pl.ds(0, META)], (((1,), (1,)), ((), ())), preferred_element_type=F32
        )
        chosen = jnp.zeros((128, 128), F32)
        for k in range(TOP):
            chosen = jnp.where(same & (wanted == codes[k : k + 1, :]), 1.0, chosen)
        return codes, chosen.astype(BF16)

    def pick(q, s, chosen):
        start, size = OUT_CUT[s]
        cols = pl.ds(start, size)
        rows = jnp.dot(chosen, tok[pl.ds(q * 128, 128), pl.ds(META + start, size)], preferred_element_type=F32)
        sel[q, :, cols] = rows.astype(BF16)
        copies = [
            send(
                sel.at[q, pl.ds(j * ROWS, ROWS), cols], xin.at[q, pl.ds(back(j) * ROWS, ROWS), cols],
                x_s.at[q, s, j], x_r.at[q, s, back(j)], in_plane(j),
            )
            for j in PEERS_PLANE
        ]
        xin[q, pl.ds(0, ROWS), cols] = sel[q, pl.ds(0, ROWS), cols]
        return copies

    def weigh(q, codes):
        scaled = jnp.zeros((128, 128), F32)
        for k in range(TOP):
            value = codes[TOP + k : TOP + k + 1, :] + codes[2 * TOP + k : 2 * TOP + k + 1, :]
            value = value + codes[3 * TOP + k : 3 * TOP + k + 1, :]
            scaled = jnp.where(same & (wanted == codes[k : k + 1, :]), value, scaled)
        turned = jnp.transpose(scaled)
        first = turned.astype(BF16)
        second = (turned - first.astype(F32)).astype(BF16)
        third = (turned - first.astype(F32) - second.astype(F32)).astype(BF16)
        mix[q, 0] = first
        mix[q, 1] = second
        mix[q, 2] = third

    parts = range(len(BLOCK_CUT))
    for s in parts:
        forward(0, s, 0)
    for a in (3, 6):
        for s in parts:
            for entry in FAR_OUT:
                if offset(entry[0], entry[1]) in (a, -a) and entry[2] == s:
                    far[entry].wait_recv()
                    forward(offset(entry[0], entry[1]), s, 0)
    for a in (0, 3, -3):
        for s in parts:
            forward(a, s, 1)
    picked = {}
    kept_codes = []
    for q in range(2):
        for s in range(len(BLOCK_CUT)):
            arrive(q, s)
            if s == 0:
                codes, chosen = match(q)
            picked[q, s] = pick(q, s, chosen)
        kept_codes.append(codes)
    loads[3].wait()
    loads[4].wait()

    def tile(d):
        return pl.ds(pl.multiple_of(lax.rem(y + d, NY) * quarter, quarter), quarter)

    sums = [None, None]
    for q in range(2):
        sums[q] = []
        for s, (start, size) in enumerate(OUT_CUT):
            for copy in picked[q, s]:
                copy.wait_recv()
            for d in PEERS_Y + (0,):
                part = jnp.dot(
                    xin[q, :, pl.ds(start, size)], up_v[pl.ds(start, size), tile(d)], preferred_element_type=F32
                )
                if s > 0:
                    part = part + upacc[q, d]
                if s < len(OUT_CUT) - 1 or d == 0:
                    upacc[q, d] = part
                else:
                    pup[q, d] = part.astype(BF16)
                    sums[q].append(
                        send(pup.at[q, d], rup.at[q, NY - d], rs_s.at[q, d], rs_r.at[q, NY - d], along_y(d))
                    )
    for q in range(2):
        weigh(q, kept_codes[q])
    gathered = [None, None]
    for q in range(2):
        for copy in sums[q]:
            copy.wait_recv()
        upper = upacc[q, 0] + rup[q, 1].astype(F32) + rup[q, 2].astype(F32) + rup[q, 3].astype(F32)
        act[q, 0] = (upper / (1.0 + jnp.exp(-upper))).astype(BF16)
        gathered[q] = [
            send(act.at[q, 0], act.at[q, NY - d], ag_s.at[q, d], ag_r.at[q, NY - d], along_y(d)) for d in PEERS_Y
        ]
    returned = {}
    for q in range(2):
        for copy in gathered[q]:
            copy.wait_recv()
        for s in range(len(HOME_CUT)):
            cols = pl.ds(*HOME_CUT[s])
            result = jnp.dot(act[q, 0], down_v[tile(0), cols], preferred_element_type=F32)
            for r in range(1, NY):
                result = result + jnp.dot(act[q, r], down_v[tile(r), cols], preferred_element_type=F32)
            eout[q, :, cols] = result.astype(BF16)
            returned[q, s] = [
                send(
                    eout.at[q, pl.ds(j * ROWS, ROWS), cols], ret.at[q, pl.ds(back(j) * ROWS, ROWS), cols],
                    b_s.at[q, s, j], b_r.at[q, s, back(j)], in_plane(j),
                )
                for j in PEERS_PLANE
            ]
            ret[q, pl.ds(0, ROWS), cols] = eout[q, pl.ds(0, ROWS), cols]

    homeward = {}
    for q in range(2):
        for s in range(len(HOME_CUT)):
            for copy in returned[q, s]:
                copy.wait_recv()
            cols = pl.ds(*HOME_CUT[s])
            rows = ret[q, :, cols]
            part = jnp.dot(mix[q, 0], rows, preferred_element_type=F32)
            part = part + jnp.dot(mix[q, 1], rows, preferred_element_type=F32)
            part = part + jnp.dot(mix[q, 2], rows, preferred_element_type=F32)
            par32[q, :, cols] = part
            par[pl.ds(q * 128, 128), cols] = part.astype(BF16)
            for i, entry in enumerate(NEAR_HOME):
                o = offset(entry[0], entry[1])
                if PLACE[o] // 8 == q and entry[2] == s:
                    homeward[entry] = send(
                        par.at[block(o), cols], brecv.at[i, :, cols], bn_s.at[i], bn_r.at[i], along_z(-entry[1])
                    )
    last = {}

    def group(a, s):
        chunk, start = divmod(PLACE[a] * ROWS, 128)
        cols = pl.ds(*HOME_CUT[s])
        value = par32[chunk, pl.ds(start, ROWS), cols]
        for i, entry in enumerate(NEAR_HOME):
            if entry[0] == a and entry[2] == s:
                homeward[entry].wait_recv()
                value = value + brecv[i, :, cols].astype(F32)
        for i, entry in enumerate(FAR_HOME):
            if entry[0] == a and entry[2] == s:
                last[entry].wait_recv()
                value = value + qr[i, :, cols].astype(F32)
        return value

    def homewards(a, s):
        value = group(a, s)
        cols = pl.ds(*HOME_CUT[s])
        for i, entry in enumerate(FAR_HOME):
            if offset(entry[0], entry[1]) == a and entry[2] == s:
                qs[i, :, cols] = value.astype(BF16)
                last[entry] = send(
                    qs.at[i, :, cols], qr.at[i, :, cols], q_s.at[i], q_r.at[i], along_z(-entry[1])
                )

    for a in sorted({abs(offset(a, b)) for a, b, _ in FAR_HOME}, reverse=True):
        for s in range(len(HOME_CUT)):
            homewards(a, s)
            homewards(-a, s)
    for s in range(len(HOME_CUT)):
        out_ref[:, pl.ds(*HOME_CUT[s])] = group(0, s).astype(BF16)
    for copy in live:
        copy.wait_send()


def body(tokens, up_weight, down_weight, expert_ids, route_weight):
    width = tokens.shape[1]
    hidden = up_weight.shape[2]
    quarter = hidden // NY
    dma = pltpu.SemaphoreType.DMA
    vmem = pl.BlockSpec(memory_space=pltpu.VMEM)
    hbm = pl.BlockSpec(memory_space=pltpu.HBM)
    scratch = [
        pltpu.VMEM((TOP, ROWS), jnp.int32),
        pltpu.VMEM((TOP, ROWS), F32),
        pltpu.VMEM((width, hidden), BF16),
        pltpu.VMEM((hidden, width), BF16),
        pltpu.VMEM((256, META + width), BF16),
        pltpu.VMEM((2, 128, width), BF16),
        pltpu.VMEM((2, 128, width), BF16),
        pltpu.VMEM((2, NY, 128, quarter), F32),
        pltpu.VMEM((2, NY, 128, quarter), BF16),
        pltpu.VMEM((2, NY, 128, quarter), BF16),
        pltpu.VMEM((2, NY, 128, quarter), BF16),
        pltpu.VMEM((2, 128, width), BF16),
        pltpu.VMEM((2, 128, width), BF16),
        pltpu.VMEM((2, 3, 128, 128), BF16),
        pltpu.VMEM((256, width), BF16),
        pltpu.VMEM((2, 128, width), F32),
        pltpu.VMEM((len(NEAR_HOME), ROWS, width), BF16),
        pltpu.VMEM((len(FAR_HOME), ROWS, width), BF16),
        pltpu.VMEM((len(FAR_HOME), ROWS, width), BF16),
        dma((5,)),
        dma((len(FAR_OUT),)), dma((len(FAR_OUT),)),
        dma((len(NEAR_OUT),)), dma((len(NEAR_OUT),)),
        dma((2, 2, PLANE)), dma((2, 2, PLANE)),
        dma((2, NY)), dma((2, NY)),
        dma((2, NY)), dma((2, NY)),
        dma((2, 2, PLANE)), dma((2, 2, PLANE)),
        dma((len(NEAR_HOME),)), dma((len(NEAR_HOME),)),
        dma((len(FAR_HOME),)), dma((len(FAR_HOME),)),
    ]
    return pl.pallas_call(
        kernel,
        out_shape=jax.ShapeDtypeStruct(tokens.shape, BF16),
        in_specs=[hbm] * 5,
        out_specs=vmem,
        scratch_shapes=scratch,
        compiler_params=pltpu.CompilerParams(
            collective_id=0, has_side_effects=True, vmem_limit_bytes=62 * 2**20
        ),
        cost_estimate=pl.CostEstimate(flops=2 * 2 * 256 * width * hidden, bytes_accessed=4 * width * hidden, transcendentals=0),
        name="experts",
    )(tokens, up_weight[0], down_weight[0], expert_ids.T, route_weight.T)


def solution(mesh):
    placed = (
        P("ep", "sec"),
        P("ep", "sec", None),
        P("ep", None, "sec"),
        P("ep", None),
        P("ep", None),
    )
    return jax.shard_map(
        body, mesh=mesh, in_specs=placed, out_specs=P("ep", "sec"), check_vma=False
    )
```

time: 72.6 us -> 67.1 us (0.924)
  local copies, waits for them, and re-layouts: 5.73 us -> 1.36 us
  Pallas kernels: 66.6 us -> 65.6 us
    unnamed x11 -> x1, local copies, waits for them, and re-layouts: 5.73 us -> 1.36 us
    pallas_call x1, Pallas kernels: 66.6 us -> 65.6 us  [body(): pl.pallas_call(kernel, out_shape=jax.ShapeDtypeStruct(tokens.shape, BF16)...]
where the time goes in v2:
time: 67.1 us; the launch traced here: 66.9 us
  Pallas kernels  65.6 us (98%)
  local copies, waits for them, and re-layouts  1.36 us (2%)
    pallas_call x1, Pallas kernels, body(): pl.pallas_call(kernel, out_shape=jax.ShapeDtypeStruct(tokens.shape, BF16)...  65.6 us
    unnamed x1, local copies, waits for them, and re-layouts  1.36 us

profile of v2, /device:TPU:6, one launch (start us, length us, event | category | flops | bytes accessed | tf_op | source)
XLA Modules:
  0.0 66.9 jit_solution(9922892446054197353)
XLA Ops:
  0.0 65.6 %experts.1 = bf16[16,896]{1,0:T(8,128)(2,1)} custom-call(bf16[16,896]{1,0:T(8,128)(2,1)} %tok_hbm.1, bf16[896,1024]{1,0:T(8,128)(2,1)} %bitcast.4, bf16[1024,896]{1,0:T(8,128)(2,1)} %bitcast.5, s32[8,16]{1,0:T(8,128)} %bitcast.6, f32[8,16]{1,0:T(8,128)} %bitcast.7), custom_call_target="tpu_custom_call" | custom-call | flops 939524096 | bytes 3670016 | tf_op jit(solution)/shard_map/experts/pallas_call | solution.py:352
  65.6 1.4 %copy.7 = bf16[16,896]{1,0:T(8,128)(2,1)} copy(bf16[16,896]{1,0:T(8,128)(2,1)} %experts.1) | data formatting | bytes 57344

commit v3 on v2

--- a/solution.py
+++ b/solution.py
@@ -15,6 +15,7 @@
 ORDER = (-4, 5, -5, 6, -6, 7, -7, 8, 0, 1, -1, 3, -3, 2, -2, 4)
 PLACE = {o: i for i, o in enumerate(ORDER)}
 META = 128
+HALVES = 2
 BLOCK_CUT = ((0, 512), (512, 512))
 OUT_CUT = ((0, 384), (384, 512))
 HOME_CUT = ((0, 512), (512, 384))
@@ -209,9 +210,9 @@
     def tile(d):
         return pl.ds(pl.multiple_of(lax.rem(y + d, NY) * quarter, quarter), quarter)
 
-    sums = [None, None]
-    for q in range(2):
-        sums[q] = []
+    half = xin.shape[1] // HALVES
+    sums = {}
+    for q in range(2):
         for s, (start, size) in enumerate(OUT_CUT):
             for copy in picked[q, s]:
                 copy.wait_recv()
@@ -225,20 +226,30 @@
                     upacc[q, d] = part
                 else:
                     pup[q, d] = part.astype(BF16)
-                    sums[q].append(
-                        send(pup.at[q, d], rup.at[q, NY - d], rs_s.at[q, d], rs_r.at[q, NY - d], along_y(d))
-                    )
+        for h in range(HALVES):
+            rows = pl.ds(h * half, half)
+            for d in PEERS_Y:
+                sums[q, h, d] = send(
+                    pup.at[q, d, rows], rup.at[q, NY - d, rows], rs_s.at[q, h, d], rs_r.at[q, h, NY - d], along_y(d)
+                )
     for q in range(2):
         weigh(q, kept_codes[q])
-    gathered = [None, None]
-    for q in range(2):
-        for copy in sums[q]:
-            copy.wait_recv()
-        upper = upacc[q, 0] + rup[q, 1].astype(F32) + rup[q, 2].astype(F32) + rup[q, 3].astype(F32)
-        act[q, 0] = (upper / (1.0 + jnp.exp(-upper))).astype(BF16)
-        gathered[q] = [
-            send(act.at[q, 0], act.at[q, NY - d], ag_s.at[q, d], ag_r.at[q, NY - d], along_y(d)) for d in PEERS_Y
-        ]
+    gathered = [[], []]
+    for q in range(2):
+        for h in range(HALVES):
+            rows = pl.ds(h * half, half)
+            for d in PEERS_Y:
+                sums[q, h, d].wait_recv()
+            upper = upacc[q, 0, rows]
+            for r in range(1, NY):
+                upper = upper + rup[q, r, rows].astype(F32)
+            act[q, 0, rows] = (upper / (1.0 + jnp.exp(-upper))).astype(BF16)
+            gathered[q] += [
+                send(
+                    act.at[q, 0, rows], act.at[q, NY - d, rows], ag_s.at[q, h, d], ag_r.at[q, h, NY - d], along_y(d)
+                )
+                for d in PEERS_Y
+            ]
     returned = {}
     for q in range(2):
         for copy in gathered[q]:
@@ -343,15 +354,15 @@
         dma((len(FAR_OUT),)), dma((len(FAR_OUT),)),
         dma((len(NEAR_OUT),)), dma((len(NEAR_OUT),)),
         dma((2, 2, PLANE)), dma((2, 2, PLANE)),
-        dma((2, NY)), dma((2, NY)),
-        dma((2, NY)), dma((2, NY)),
+        dma((2, HALVES, NY)), dma((2, HALVES, NY)),
+        dma((2, HALVES, NY)), dma((2, HALVES, NY)),
         dma((2, 2, PLANE)), dma((2, 2, PLANE)),
         dma((len(NEAR_HOME),)), dma((len(NEAR_HOME),)),
         dma((len(FAR_HOME),)), dma((len(FAR_HOME),)),
     ]
     return pl.pallas_call(
         kernel,
-        out_shape=jax.ShapeDtypeStruct(tokens.shape, BF16),
+        out_shape=pltpu.VMEM(tokens.shape, BF16),
         in_specs=[hbm] * 5,
         out_specs=vmem,
         scratch_shapes=scratch,

time: 67.1 us -> 64.9 us (0.967)
  Pallas kernels: 65.6 us -> 64.1 us
  local copies, waits for them, and re-layouts: 1.36 us -> 0.61 us
    pallas_call x1, Pallas kernels: 65.6 us -> 64.1 us  [body(): pl.pallas_call(kernel, out_shape=pltpu.VMEM(tokens.shape, BF16), in_specs...]
    unnamed x1, local copies, waits for them, and re-layouts: 1.36 us -> 0.61 us
where the time goes in v3:
time: 64.9 us; the launch traced here: 64.8 us
  Pallas kernels  64.1 us (99%)
    pallas_call x1, Pallas kernels, body(): pl.pallas_call(kernel, out_shape=pltpu.VMEM(tokens.shape, BF16), in_specs...  64.1 us

profile of v3, /device:TPU:6, one launch (start us, length us, event | category | flops | bytes accessed | tf_op | source)
XLA Modules:
  0.0 64.8 jit_solution(425698970676408106)
XLA Ops:
  0.0 64.1 %experts.1 = bf16[16,896]{1,0:T(8,128)(2,1)S(1)} custom-call(bf16[16,896]{1,0:T(8,128)(2,1)} %tok_hbm.1, bf16[896,1024]{1,0:T(8,128)(2,1)} %bitcast.4, bf16[1024,896]{1,0:T(8,128)(2,1)} %bitcast.5, s32[8,16]{1,0:T(8,128)} %bitcast.6, f32[8,16]{1,0:T(8,128)} %bitcast.7), custom_call_target="tpu_custom_call" | custom-call | flops 939524096 | bytes 3670016 | tf_op jit(solution)/shard_map/experts/pallas_call | solution.py:363
  64.1 0.6 copy.7

commit v4 on v3

--- a/solution.py
+++ b/solution.py
@@ -88,7 +88,7 @@
     peers = [along_z(s) for s in PEERS_Z] + [in_plane(j) for j in PEERS_PLANE] + [along_y(d) for d in PEERS_Y]
     for peer in peers:
         pl.semaphore_signal(barrier, inc=1, device_id=peer, device_id_type=MESH)
-    for load in loads:
+    for load in loads[:3]:
         load.start()
 
     loads[0].wait()
@@ -113,6 +113,8 @@
         jnp.where(unit, 1.0, 0.0).astype(BF16), table, (((1,), (1,)), ((), ())), preferred_element_type=F32
     ).astype(BF16)
     loads[2].wait()
+    for load in loads[3:]:
+        load.start()
     pl.semaphore_wait(barrier, len(peers))
 
     far, near = {}, {}
@@ -317,9 +319,11 @@
         for s in range(len(HOME_CUT)):
             homewards(a, s)
             homewards(-a, s)
+    for copy in live[: -len(FAR_HOME) // 2]:
+        copy.wait_send()
     for s in range(len(HOME_CUT)):
         out_ref[:, pl.ds(*HOME_CUT[s])] = group(0, s).astype(BF16)
-    for copy in live:
+    for copy in live[-len(FAR_HOME) // 2 :]:
         copy.wait_send()
 
 

time: 64.9 us -> 64.7 us (level)
  no operation moved by 1% of the time
where the time goes in v4:
time: 64.7 us; the launch traced here: 64.5 us
  Pallas kernels  63.9 us (99%)
    pallas_call x1, Pallas kernels, body(): pl.pallas_call(kernel, out_shape=pltpu.VMEM(tokens.shape, BF16), in_specs...  63.9 us

profile of v4, /device:TPU:6, one launch (start us, length us, event | category | flops | bytes accessed | tf_op | source)
XLA Modules:
  0.0 64.5 jit_solution(4987654012046973773)
XLA Ops:
  0.0 63.9 %experts.1 = bf16[16,896]{1,0:T(8,128)(2,1)S(1)} custom-call(bf16[16,896]{1,0:T(8,128)(2,1)} %tok_hbm.1, bf16[896,1024]{1,0:T(8,128)(2,1)} %bitcast.4, bf16[1024,896]{1,0:T(8,128)(2,1)} %bitcast.5, s32[8,16]{1,0:T(8,128)} %bitcast.6, f32[8,16]{1,0:T(8,128)} %bitcast.7), custom_call_target="tpu_custom_call" | custom-call | flops 939524096 | bytes 3670016 | tf_op jit(solution)/shard_map/experts/pallas_call | solution.py:367
  63.9 0.6 copy.7
